TPU v7x, 256 devices: a whole 4x4x8 slice. The times are simulated.
256 devices in a mesh: section: 8 (over z_hi, y), dp: 32 (over z_lo, x, core).
Axes of the slice: x: 4, y: 4, z: 8 (z_hi: 2, z_lo: 4; z = z_hi * 4 + z_lo), core: 2. Of those that a mesh axis runs over, the one named last changes fastest.
Arguments:
- inputs: bfloat16 [2, 4096, 2048], P(None, 'dp'), may hold values from -6 to 6
- cotangent: bfloat16 [2, 4096, 2048], P(None, 'dp'), may hold values from -6 to 6
- weights: bfloat16 [8, 2048, 2048], P('section'), may hold values from -0.125 to 0.125
- gains: float32 [8, 2048], P('section'), may hold values from 0.1 to 1.9
Outputs:
- grad_input: bfloat16 [8, 2, 4096, 2048], P('section', None, 'dp')
- weight_grad: float32 [8, 2048, 2048], P('section', 'dp')
- gain_grad: float32 [8, 2048], P('section')
All inputs are finite; a program needn't handle non-finite values.
Results may differ from a plain program's by a relative error of at most 0.033.
Values may be sent and summed in bfloat16 or wider, within the bound.
A program may use at most 128 MiB of HBM per device.

v0:
```python
import math

import jax
import jax.numpy as jnp
from jax import lax
from jax.sharding import PartitionSpec as P

eps = 1e-05


def shifted(block, axis, distance):
    devices = range(lax.axis_size(axis))
    route = [(i - distance, i) for i in devices if i - distance in devices]
    return lax.ppermute(block, axis, route)


def normalize(act, gain):
    af = act.astype(jnp.float32)
    radius = jnp.sqrt(jnp.mean(af * af, axis=-1, keepdims=True) + eps)
    normed = (af / radius * gain).astype(jnp.bfloat16)
    return (af, radius, normed)


def on_device(inputs, cotangent, weights, gains):
    weight = weights[0]
    gain = gains[0]
    micro, tok_rows, width = inputs.shape
    section_id = lax.axis_index("section")
    n_section = lax.axis_size("section")
    n_data = lax.axis_size("dp")
    total_steps = micro + n_section - 1
    scale = 1.0 / math.sqrt(micro * tok_rows * n_data)

    def forward_step(step, carry):
        outgoing, stored = carry
        arrived = shifted(outgoing, "section", 1)
        which = step - section_id
        valid = (which >= 0) & (which < micro)
        slot = jnp.clip(which, 0, micro - 1)
        first = lax.dynamic_index_in_dim(inputs, slot, 0, keepdims=False)
        act = jnp.where(section_id == 0, first, arrived)

        def forward_active(state):
            act_in, kept = state
            af, radius, normed = normalize(act_in, gain)
            result = (af + jnp.dot(normed, weight, preferred_element_type=jnp.float32)).astype(
                jnp.bfloat16
            )
            return (result, lax.dynamic_update_index_in_dim(kept, act_in, slot, 0))

        def forward_resting(state):
            return (jnp.zeros_like(state[0]), state[1])

        return lax.cond(valid, forward_active, forward_resting, (act, stored))

    empty = jnp.zeros((tok_rows, width), jnp.bfloat16)
    stored = jnp.zeros((micro, tok_rows, width), jnp.bfloat16)
    outgoing, stored = lax.fori_loop(0, total_steps, forward_step, (empty, stored))
    w_total = jnp.zeros((width, width), jnp.float32)

    def backward_step(step, carry):
        outgoing, grad_store, upstream_store, w_acc, g_acc = carry
        arrived = shifted(outgoing, "section", -1)
        which = step - (n_section - 1 - section_id)
        valid = (which >= 0) & (which < micro)
        slot = jnp.clip(which, 0, micro - 1)
        given = lax.dynamic_index_in_dim(cotangent, slot, 0, keepdims=False)
        upstream = jnp.where(section_id == n_section - 1, given, arrived)

        def backward_active(state):
            upper, grads, uppers, wsum, gsum = state
            act_in = lax.dynamic_index_in_dim(stored, slot, 0, keepdims=False)
            af, radius, normed = normalize(act_in, gain)
            dnorm = lax.dot_general(
                upper, weight, (((1,), (1,)), ((), ())), preferred_element_type=jnp.float32
            )
            gdn = gain * dnorm
            back = (
                upper.astype(jnp.float32)
                + gdn / radius
                - af * jnp.sum(gdn * af, axis=-1, keepdims=True) / (width * radius**3)
            )
            lower = back.astype(jnp.bfloat16)
            gsum = gsum + jnp.sum(dnorm * af / radius, axis=0)
            grads = lax.dynamic_update_index_in_dim(grads, lower, slot, 0)
            wsum = wsum + lax.dot_general(
                normed, upper, (((0,), (0,)), ((), ())), preferred_element_type=jnp.float32
            )
            return (lower, grads, uppers, wsum, gsum)

        def backward_resting(state):
            return (jnp.zeros_like(state[0]),) + state[1:]

        return lax.cond(
            valid,
            backward_active,
            backward_resting,
            (upstream, grad_store, upstream_store, w_acc, g_acc),
        )

    grad_store = jnp.zeros((micro, tok_rows, width), jnp.bfloat16)
    upstream_store = jnp.zeros((micro, tok_rows, width), jnp.bfloat16)
    g_start = jnp.zeros((width,), jnp.float32)
    carry = lax.fori_loop(
        0, total_steps, backward_step, (empty, grad_store, upstream_store, w_total, g_start)
    )
    outgoing, grad_store, upstream_store, w_total, g_local = carry
    w_share = lax.psum_scatter(
        w_total.astype(jnp.bfloat16), "dp", scatter_dimension=0, tiled=True
    ).astype(jnp.float32)
    g_total = lax.psum(g_local, "dp")
    return (grad_store[None], (w_share * scale)[None], (g_total * scale)[None])


def solution(mesh):
    return jax.shard_map(
        on_device,
        mesh=mesh,
        in_specs=(
            P(None, "dp", None),
            P(None, "dp", None),
            P("section", None, None),
            P("section", None),
        ),
        out_specs=(P("section", None, "dp", None), P("section", "dp", None), P("section", None)),
        check_vma=False,
    )
```

profile of v0, /device:TPU:1, one launch (start us, length us, event | category | flops | bytes accessed | tf_op | source)
XLA Modules:
  0.0 748.4 jit_solution(5835830338919953128)
XLA Ops:
  8.2 152.4 %while.40 = (s32[]{:T(128)}, bf16[128,2048]{1,0:T(8,128)(2,1)}, bf16[2,128,2048]{2,1,0:T(8,128)(2,1)S(1)}, s32[]{:T(128)}, pred[]{:T(512)}, /*index=5*/bf16[2,12...) while((s32[]{:T(128)}, bf16[128,2048]{1,0:T(8,128)(2,1)}, ...), condition=%wide.region_4.5_spmd, body=%wide.region_0.4_spmd.sunk | while | flops 1076625536 | bytes 14166312 | solution.py:58
  12.3 10.8 %collective-permute-done = bf16[128,2048]{1,0:T(8,128)(2,1)S(1)} collective-permute-done((bf16[128,2048]{1,0:T(8,128)(2,1)}, bf16[128,2048]{1,0:T(8,128)(2,1)S(1)}, u32[]{:S(2)}, u32[]{:S(2)}) %collective-permute-start) | collective-permute-done | bytes 524320 | tf_op jit(solution)/shard_map/while/body/eval_jaxpr/ppermute | solution.py:14
  23.1 6.9 conditional.4
  31.4 10.2 %collective-permute-done = bf16[128,2048]{1,0:T(8,128)(2,1)S(1)} collective-permute-done((bf16[128,2048]{1,0:T(8,128)(2,1)}, bf16[128,2048]{1,0:T(8,128)(2,1)S(1)}, u32[]{:S(2)}, u32[]{:S(2)}) %collective-permute-start) | collective-permute-done | bytes 524320 | tf_op jit(solution)/shard_map/while/body/eval_jaxpr/ppermute | solution.py:14
  41.6 6.9 conditional.4
  52.6 9.3 %collective-permute-done = bf16[128,2048]{1,0:T(8,128)(2,1)S(1)} collective-permute-done((bf16[128,2048]{1,0:T(8,128)(2,1)}, bf16[128,2048]{1,0:T(8,128)(2,1)S(1)}, u32[]{:S(2)}, u32[]{:S(2)}) %collective-permute-start) | collective-permute-done | bytes 524320 | tf_op jit(solution)/shard_map/while/body/eval_jaxpr/ppermute | solution.py:14
  62.7 10.1 %collective-permute-start = (bf16[128,2048]{1,0:T(8,128)(2,1)}, bf16[128,2048]{1,0:T(8,128)(2,1)S(1)}, u32[]{:S(2)}, u32[]{:S(2)}) collective-permute-start(bf16[128,2048]{1,0:T(8,128)(2,1)} %get-tuple-element.786), channel_id=1, source_target_pairs={{0,32},{32,64},{64,96},{96,128},{128,160},{160,192},{192,224},{1,3... | collective-permute-start | bytes 1572872 | tf_op jit(solution)/shard_map/while/body/eval_jaxpr/ppermute | solution.py:14
  72.9 8.4 %collective-permute-done = bf16[128,2048]{1,0:T(8,128)(2,1)S(1)} collective-permute-done((bf16[128,2048]{1,0:T(8,128)(2,1)}, bf16[128,2048]{1,0:T(8,128)(2,1)S(1)}, u32[]{:S(2)}, u32[]{:S(2)}) %collective-permute-start) | collective-permute-done | bytes 524320 | tf_op jit(solution)/shard_map/while/body/eval_jaxpr/ppermute | solution.py:14
  86.1 7.4 collective-permute-done
  94.4 7.7 %collective-permute-start = (bf16[128,2048]{1,0:T(8,128)(2,1)}, bf16[128,2048]{1,0:T(8,128)(2,1)S(1)}, u32[]{:S(2)}, u32[]{:S(2)}) collective-permute-start(bf16[128,2048]{1,0:T(8,128)(2,1)} %get-tuple-element.786), channel_id=1, source_target_pairs={{0,32},{32,64},{64,96},{96,128},{128,160},{160,192},{192,224},{1,3... | collective-permute-start | bytes 1572872 | tf_op jit(solution)/shard_map/while/body/eval_jaxpr/ppermute | solution.py:14
  109.4 9.5 %collective-permute-start = (bf16[128,2048]{1,0:T(8,128)(2,1)}, bf16[128,2048]{1,0:T(8,128)(2,1)S(1)}, u32[]{:S(2)}, u32[]{:S(2)}) collective-permute-start(bf16[128,2048]{1,0:T(8,128)(2,1)} %get-tuple-element.786), channel_id=1, source_target_pairs={{0,32},{32,64},{64,96},{96,128},{128,160},{160,192},{192,224},{1,3... | collective-permute-start | bytes 1572872 | tf_op jit(solution)/shard_map/while/body/eval_jaxpr/ppermute | solution.py:14
  118.9 6.4 collective-permute-done
  126.1 10.1 %collective-permute-start = (bf16[128,2048]{1,0:T(8,128)(2,1)}, bf16[128,2048]{1,0:T(8,128)(2,1)S(1)}, u32[]{:S(2)}, u32[]{:S(2)}) collective-permute-start(bf16[128,2048]{1,0:T(8,128)(2,1)} %get-tuple-element.786), channel_id=1, source_target_pairs={{0,32},{32,64},{64,96},{96,128},{128,160},{160,192},{192,224},{1,3... | collective-permute-start | bytes 1572872 | tf_op jit(solution)/shard_map/while/body/eval_jaxpr/ppermute | solution.py:14
  143.5 9.9 %collective-permute-start = (bf16[128,2048]{1,0:T(8,128)(2,1)}, bf16[128,2048]{1,0:T(8,128)(2,1)S(1)}, u32[]{:S(2)}, u32[]{:S(2)}) collective-permute-start(bf16[128,2048]{1,0:T(8,128)(2,1)} %get-tuple-element.786), channel_id=1, source_target_pairs={{0,32},{32,64},{64,96},{96,128},{128,160},{160,192},{192,224},{1,3... | collective-permute-start | bytes 1572872 | tf_op jit(solution)/shard_map/while/body/eval_jaxpr/ppermute | solution.py:14
  162.5 7.9 %broadcast_in_dim.29 = f32[2048,2048]{1,0:T(8,128)} broadcast(f32[]{:T(128)} %constant.149.clone.1), dimensions={} | broadcast | bytes 16777220 | tf_op jit(solution)/shard_map/broadcast_in_dim | solution.py:59
  170.4 274.3 %while.41 = (s32[]{:T(128)}, bf16[128,2048]{1,0:T(8,128)(2,1)}, bf16[2,128,2048]{2,1,0:T(8,128)(2,1)}, f32[2048,2048]{1,0:T(8,128)}, f32[2048]{0:T(1024)S(1)}, /...) while((s32[]{:T(128)}, bf16[128,2048]{1,0:T(8,128)(2,1)}, ...), condition=%wide.region_11.12_spmd, body=%wide.region_5.11_spmd.sunk | while | flops 2157969920 | bytes 186709456 | solution.py:104
  171.7 21.4 %collective-permute-done.1 = bf16[128,2048]{1,0:T(8,128)(2,1)S(1)} collective-permute-done((bf16[128,2048]{1,0:T(8,128)(2,1)}, bf16[128,2048]{1,0:T(8,128)(2,1)S(1)}, u32[]{:S(2)}, u32[]{:S(2)}) %collective-permute-start.1) | collective-permute-done | bytes 524320 | tf_op jit(solution)/shard_map/while/body/eval_jaxpr/ppermute | solution.py:14
  195.2 15.2 %collective-permute-done.1 = bf16[128,2048]{1,0:T(8,128)(2,1)S(1)} collective-permute-done((bf16[128,2048]{1,0:T(8,128)(2,1)}, bf16[128,2048]{1,0:T(8,128)(2,1)S(1)}, u32[]{:S(2)}, u32[]{:S(2)}) %collective-permute-start.1) | collective-permute-done | bytes 524320 | tf_op jit(solution)/shard_map/while/body/eval_jaxpr/ppermute | solution.py:14
  212.6 15.3 %collective-permute-done.1 = bf16[128,2048]{1,0:T(8,128)(2,1)S(1)} collective-permute-done((bf16[128,2048]{1,0:T(8,128)(2,1)}, bf16[128,2048]{1,0:T(8,128)(2,1)S(1)}, u32[]{:S(2)}, u32[]{:S(2)}) %collective-permute-start.1) | collective-permute-done | bytes 524320 | tf_op jit(solution)/shard_map/while/body/eval_jaxpr/ppermute | solution.py:14
  230.0 15.5 %collective-permute-done.1 = bf16[128,2048]{1,0:T(8,128)(2,1)S(1)} collective-permute-done((bf16[128,2048]{1,0:T(8,128)(2,1)}, bf16[128,2048]{1,0:T(8,128)(2,1)S(1)}, u32[]{:S(2)}, u32[]{:S(2)}) %collective-permute-start.1) | collective-permute-done | bytes 524320 | tf_op jit(solution)/shard_map/while/body/eval_jaxpr/ppermute | solution.py:14
  247.7 17.1 %collective-permute-done.1 = bf16[128,2048]{1,0:T(8,128)(2,1)S(1)} collective-permute-done((bf16[128,2048]{1,0:T(8,128)(2,1)}, bf16[128,2048]{1,0:T(8,128)(2,1)S(1)}, u32[]{:S(2)}, u32[]{:S(2)}) %collective-permute-start.1) | collective-permute-done | bytes 524320 | tf_op jit(solution)/shard_map/while/body/eval_jaxpr/ppermute | solution.py:14
  266.9 18.2 %collective-permute-done.1 = bf16[128,2048]{1,0:T(8,128)(2,1)S(1)} collective-permute-done((bf16[128,2048]{1,0:T(8,128)(2,1)}, bf16[128,2048]{1,0:T(8,128)(2,1)S(1)}, u32[]{:S(2)}, u32[]{:S(2)}) %collective-permute-start.1) | collective-permute-done | bytes 524320 | tf_op jit(solution)/shard_map/while/body/eval_jaxpr/ppermute | solution.py:14
  287.3 19.4 %collective-permute-done.1 = bf16[128,2048]{1,0:T(8,128)(2,1)S(1)} collective-permute-done((bf16[128,2048]{1,0:T(8,128)(2,1)}, bf16[128,2048]{1,0:T(8,128)(2,1)S(1)}, u32[]{:S(2)}, u32[]{:S(2)}) %collective-permute-start.1) | collective-permute-done | bytes 524320 | tf_op jit(solution)/shard_map/while/body/eval_jaxpr/ppermute | solution.py:14
  308.9 85.7 %collective-permute-done.1 = bf16[128,2048]{1,0:T(8,128)(2,1)S(1)} collective-permute-done((bf16[128,2048]{1,0:T(8,128)(2,1)}, bf16[128,2048]{1,0:T(8,128)(2,1)S(1)}, u32[]{:S(2)}, u32[]{:S(2)}) %collective-permute-start.1) | collective-permute-done | bytes 524320 | tf_op jit(solution)/shard_map/while/body/eval_jaxpr/ppermute | solution.py:14
  394.5 16.9 %conditional.5 = (bf16[128,2048]{1,0:T(8,128)(2,1)}, bf16[2,128,2048]{2,1,0:T(8,128)(2,1)}, f32[2048,2048]{1,0:T(8,128)}, f32[2048]{0:T(1024)S(1)}) conditional(s32[]{:T(128)} %convert_element_type.87, (bf16[2,128,2048]{2,1,0:T(8,128)(2,1)}, f32[2048,2048]{1,0:T(8,128)}, f32[2048]{0:T(1024)S(1)}) %tuple.105, (pred[]{:T(512)}, s32[]{:T(128)}, ...), branch_computations={%region_6.6_spmd, %region_7.10_spmd} | conditional | flops 2157969920 | bytes 184611968 | solution.py:94
  394.8 6.6 fusion.15
  412.8 14.9 %collective-permute-done.1 = bf16[128,2048]{1,0:T(8,128)(2,1)S(1)} collective-permute-done((bf16[128,2048]{1,0:T(8,128)(2,1)}, bf16[128,2048]{1,0:T(8,128)(2,1)S(1)}, u32[]{:S(2)}, u32[]{:S(2)}) %collective-permute-start.1) | collective-permute-done | bytes 524320 | tf_op jit(solution)/shard_map/while/body/eval_jaxpr/ppermute | solution.py:14
  427.7 16.9 %conditional.5 = (bf16[128,2048]{1,0:T(8,128)(2,1)}, bf16[2,128,2048]{2,1,0:T(8,128)(2,1)}, f32[2048,2048]{1,0:T(8,128)}, f32[2048]{0:T(1024)S(1)}) conditional(s32[]{:T(128)} %convert_element_type.87, (bf16[2,128,2048]{2,1,0:T(8,128)(2,1)}, f32[2048,2048]{1,0:T(8,128)}, f32[2048]{0:T(1024)S(1)}) %tuple.105, (pred[]{:T(512)}, s32[]{:T(128)}, ...), branch_computations={%region_6.6_spmd, %region_7.10_spmd} | conditional | flops 2157969920 | bytes 184611968 | solution.py:94
  428.0 6.6 fusion.15
  444.6 9.1 %convert_element_type.61 = bf16[2048,2048]{1,0:T(8,128)(2,1)} convert(f32[2048,2048]{1,0:T(8,128)} %get-tuple-element.585) | non-fusion elementwise | flops 4194304 | bytes 25165824 | tf_op jit(solution)/shard_map/convert_element_type | solution.py:109
  453.8 188.6 %psum.7 = f32[2048]{0:T(1024)S(1)} all-reduce(f32[2048]{0:T(1024)S(1)} %get-tuple-element.586), channel_id=1, replica_groups=mesh['section'=8,'dp'=32] {'dp'}, use_global_device_ids=true, to_apply=%region_13.14 | all-reduce | flops 2048 | bytes 16384 | tf_op jit(solution)/shard_map/psum | solution.py:111
  642.9 96.9 %reduce-scatter.2.cloned.1.call-done = bf16[64,2048]{1,0:T(8,128)(2,1)} async-done(((bf16[2048,2048]{1,0:T(8,128)(2,1)}), bf16[64,2048]{1,0:T(8,128)(2,1)}) %reduce-scatter.2.cloned.1.call-update) | async-done | bytes 262160 | tf_op jit(solution)/shard_map/reduce_scatter | solution.py:108
  (85 shorter events, 107.5 us)
Async XLA Ops:
  7.2 732.6 %reduce-scatter.2.cloned.1.call-start = ((), (), s32[]{:S(2)}) async-start(), calls=%async_computation.1 | async-start | bytes 8650752 | tf_op jit(solution)/shard_map/reduce_scatter | solution.py:108
  8.2 14.9 %collective-permute-start = (bf16[128,2048]{1,0:T(8,128)(2,1)}, bf16[128,2048]{1,0:T(8,128)(2,1)S(1)}, u32[]{:S(2)}, u32[]{:S(2)}) collective-permute-start(bf16[128,2048]{1,0:T(8,128)(2,1)} %get-tuple-element.786), channel_id=1, source_target_pairs={{0,32},{32,64},{64,96},{96,128},{128,160},{160,192},{192,224},{1,3... | collective-permute-start | bytes 1572872 | tf_op jit(solution)/shard_map/while/body/eval_jaxpr/ppermute | solution.py:14
  30.1 11.5 %collective-permute-start = (bf16[128,2048]{1,0:T(8,128)(2,1)}, bf16[128,2048]{1,0:T(8,128)(2,1)S(1)}, u32[]{:S(2)}, u32[]{:S(2)}) collective-permute-start(bf16[128,2048]{1,0:T(8,128)(2,1)} %get-tuple-element.786), channel_id=1, source_target_pairs={{0,32},{32,64},{64,96},{96,128},{128,160},{160,192},{192,224},{1,3... | collective-permute-start | bytes 1572872 | tf_op jit(solution)/shard_map/while/body/eval_jaxpr/ppermute | solution.py:14
  48.6 13.3 %collective-permute-start = (bf16[128,2048]{1,0:T(8,128)(2,1)}, bf16[128,2048]{1,0:T(8,128)(2,1)S(1)}, u32[]{:S(2)}, u32[]{:S(2)}) collective-permute-start(bf16[128,2048]{1,0:T(8,128)(2,1)} %get-tuple-element.786), channel_id=1, source_target_pairs={{0,32},{32,64},{64,96},{96,128},{128,160},{160,192},{192,224},{1,3... | collective-permute-start | bytes 1572872 | tf_op jit(solution)/shard_map/while/body/eval_jaxpr/ppermute | solution.py:14
  62.7 18.5 %collective-permute-start = (bf16[128,2048]{1,0:T(8,128)(2,1)}, bf16[128,2048]{1,0:T(8,128)(2,1)S(1)}, u32[]{:S(2)}, u32[]{:S(2)}) collective-permute-start(bf16[128,2048]{1,0:T(8,128)(2,1)} %get-tuple-element.786), channel_id=1, source_target_pairs={{0,32},{32,64},{64,96},{96,128},{128,160},{160,192},{192,224},{1,3... | collective-permute-start | bytes 1572872 | tf_op jit(solution)/shard_map/while/body/eval_jaxpr/ppermute | solution.py:14
  82.1 11.5 %collective-permute-start = (bf16[128,2048]{1,0:T(8,128)(2,1)}, bf16[128,2048]{1,0:T(8,128)(2,1)S(1)}, u32[]{:S(2)}, u32[]{:S(2)}) collective-permute-start(bf16[128,2048]{1,0:T(8,128)(2,1)} %get-tuple-element.786), channel_id=1, source_target_pairs={{0,32},{32,64},{64,96},{96,128},{128,160},{160,192},{192,224},{1,3... | collective-permute-start | bytes 1572872 | tf_op jit(solution)/shard_map/while/body/eval_jaxpr/ppermute | solution.py:14
  94.4 14.1 %collective-permute-start = (bf16[128,2048]{1,0:T(8,128)(2,1)}, bf16[128,2048]{1,0:T(8,128)(2,1)S(1)}, u32[]{:S(2)}, u32[]{:S(2)}) collective-permute-start(bf16[128,2048]{1,0:T(8,128)(2,1)} %get-tuple-element.786), channel_id=1, source_target_pairs={{0,32},{32,64},{64,96},{96,128},{128,160},{160,192},{192,224},{1,3... | collective-permute-start | bytes 1572872 | tf_op jit(solution)/shard_map/while/body/eval_jaxpr/ppermute | solution.py:14
  109.4 15.9 %collective-permute-start = (bf16[128,2048]{1,0:T(8,128)(2,1)}, bf16[128,2048]{1,0:T(8,128)(2,1)S(1)}, u32[]{:S(2)}, u32[]{:S(2)}) collective-permute-start(bf16[128,2048]{1,0:T(8,128)(2,1)} %get-tuple-element.786), channel_id=1, source_target_pairs={{0,32},{32,64},{64,96},{96,128},{128,160},{160,192},{192,224},{1,3... | collective-permute-start | bytes 1572872 | tf_op jit(solution)/shard_map/while/body/eval_jaxpr/ppermute | solution.py:14
  126.1 16.5 %collective-permute-start = (bf16[128,2048]{1,0:T(8,128)(2,1)}, bf16[128,2048]{1,0:T(8,128)(2,1)S(1)}, u32[]{:S(2)}, u32[]{:S(2)}) collective-permute-start(bf16[128,2048]{1,0:T(8,128)(2,1)} %get-tuple-element.786), channel_id=1, source_target_pairs={{0,32},{32,64},{64,96},{96,128},{128,160},{160,192},{192,224},{1,3... | collective-permute-start | bytes 1572872 | tf_op jit(solution)/shard_map/while/body/eval_jaxpr/ppermute | solution.py:14
  143.5 16.3 %collective-permute-start = (bf16[128,2048]{1,0:T(8,128)(2,1)}, bf16[128,2048]{1,0:T(8,128)(2,1)S(1)}, u32[]{:S(2)}, u32[]{:S(2)}) collective-permute-start(bf16[128,2048]{1,0:T(8,128)(2,1)} %get-tuple-element.786), channel_id=1, source_target_pairs={{0,32},{32,64},{64,96},{96,128},{128,160},{160,192},{192,224},{1,3... | collective-permute-start | bytes 1572872 | tf_op jit(solution)/shard_map/while/body/eval_jaxpr/ppermute | solution.py:14
  160.6 9.8 %copy-start.2 = (bf16[2,128,2048]{2,1,0:T(8,128)(2,1)S(1)}, bf16[2,128,2048]{2,1,0:T(8,128)(2,1)}, u32[]{:S(2)}) copy-start(bf16[2,128,2048]{2,1,0:T(8,128)(2,1)} %param.13) | copy-start | bytes 3145732
  160.6 9.8 %copy-start.3 = (f32[1,2048]{1,0:T(1,128)S(1)}, f32[1,2048]{1,0:T(1,128)}, u32[]{:S(2)}) copy-start(f32[1,2048]{1,0:T(1,128)} %get-tuple-element.854) | copy-start | bytes 24580
  170.4 22.7 %collective-permute-start.1 = (bf16[128,2048]{1,0:T(8,128)(2,1)}, bf16[128,2048]{1,0:T(8,128)(2,1)S(1)}, u32[]{:S(2)}, u32[]{:S(2)}) collective-permute-start(bf16[128,2048]{1,0:T(8,128)(2,1)} %get-tuple-element.822), channel_id=1, source_target_pairs={{32,0},{64,32},{96,64},{128,96},{160,128},{192,160},{224,192},{33,... | collective-permute-start | bytes 1572872 | tf_op jit(solution)/shard_map/while/body/eval_jaxpr/ppermute | solution.py:14
  193.9 16.5 %collective-permute-start.1 = (bf16[128,2048]{1,0:T(8,128)(2,1)}, bf16[128,2048]{1,0:T(8,128)(2,1)S(1)}, u32[]{:S(2)}, u32[]{:S(2)}) collective-permute-start(bf16[128,2048]{1,0:T(8,128)(2,1)} %get-tuple-element.822), channel_id=1, source_target_pairs={{32,0},{64,32},{96,64},{128,96},{160,128},{192,160},{224,192},{33,... | collective-permute-start | bytes 1572872 | tf_op jit(solution)/shard_map/while/body/eval_jaxpr/ppermute | solution.py:14
  211.3 16.6 %collective-permute-start.1 = (bf16[128,2048]{1,0:T(8,128)(2,1)}, bf16[128,2048]{1,0:T(8,128)(2,1)S(1)}, u32[]{:S(2)}, u32[]{:S(2)}) collective-permute-start(bf16[128,2048]{1,0:T(8,128)(2,1)} %get-tuple-element.822), channel_id=1, source_target_pairs={{32,0},{64,32},{96,64},{128,96},{160,128},{192,160},{224,192},{33,... | collective-permute-start | bytes 1572872 | tf_op jit(solution)/shard_map/while/body/eval_jaxpr/ppermute | solution.py:14
  228.7 16.8 %collective-permute-start.1 = (bf16[128,2048]{1,0:T(8,128)(2,1)}, bf16[128,2048]{1,0:T(8,128)(2,1)S(1)}, u32[]{:S(2)}, u32[]{:S(2)}) collective-permute-start(bf16[128,2048]{1,0:T(8,128)(2,1)} %get-tuple-element.822), channel_id=1, source_target_pairs={{32,0},{64,32},{96,64},{128,96},{160,128},{192,160},{224,192},{33,... | collective-permute-start | bytes 1572872 | tf_op jit(solution)/shard_map/while/body/eval_jaxpr/ppermute | solution.py:14
  246.4 18.4 %collective-permute-start.1 = (bf16[128,2048]{1,0:T(8,128)(2,1)}, bf16[128,2048]{1,0:T(8,128)(2,1)S(1)}, u32[]{:S(2)}, u32[]{:S(2)}) collective-permute-start(bf16[128,2048]{1,0:T(8,128)(2,1)} %get-tuple-element.822), channel_id=1, source_target_pairs={{32,0},{64,32},{96,64},{128,96},{160,128},{192,160},{224,192},{33,... | collective-permute-start | bytes 1572872 | tf_op jit(solution)/shard_map/while/body/eval_jaxpr/ppermute | solution.py:14
  265.6 19.5 %collective-permute-start.1 = (bf16[128,2048]{1,0:T(8,128)(2,1)}, bf16[128,2048]{1,0:T(8,128)(2,1)S(1)}, u32[]{:S(2)}, u32[]{:S(2)}) collective-permute-start(bf16[128,2048]{1,0:T(8,128)(2,1)} %get-tuple-element.822), channel_id=1, source_target_pairs={{32,0},{64,32},{96,64},{128,96},{160,128},{192,160},{224,192},{33,... | collective-permute-start | bytes 1572872 | tf_op jit(solution)/shard_map/while/body/eval_jaxpr/ppermute | solution.py:14
  286.0 20.7 %collective-permute-start.1 = (bf16[128,2048]{1,0:T(8,128)(2,1)}, bf16[128,2048]{1,0:T(8,128)(2,1)S(1)}, u32[]{:S(2)}, u32[]{:S(2)}) collective-permute-start(bf16[128,2048]{1,0:T(8,128)(2,1)} %get-tuple-element.822), channel_id=1, source_target_pairs={{32,0},{64,32},{96,64},{128,96},{160,128},{192,160},{224,192},{33,... | collective-permute-start | bytes 1572872 | tf_op jit(solution)/shard_map/while/body/eval_jaxpr/ppermute | solution.py:14
  307.6 87.0 %collective-permute-start.1 = (bf16[128,2048]{1,0:T(8,128)(2,1)}, bf16[128,2048]{1,0:T(8,128)(2,1)S(1)}, u32[]{:S(2)}, u32[]{:S(2)}) collective-permute-start(bf16[128,2048]{1,0:T(8,128)(2,1)} %get-tuple-element.822), channel_id=1, source_target_pairs={{32,0},{64,32},{96,64},{128,96},{160,128},{192,160},{224,192},{33,... | collective-permute-start | bytes 1572872 | tf_op jit(solution)/shard_map/while/body/eval_jaxpr/ppermute | solution.py:14
  394.5 8.3 %copy-start = (f32[2048,2048]{1,0:T(8,128)S(1)}, f32[2048,2048]{1,0:T(8,128)}, u32[]{:S(2)}) copy-start(f32[2048,2048]{1,0:T(8,128)} %get-tuple-element.558) | copy-start | bytes 50331652 | tf_op jit(solution)/shard_map/while/body/eval_jaxpr/cond
  405.7 5.7 copy-start.1
  411.5 16.2 %collective-permute-start.1 = (bf16[128,2048]{1,0:T(8,128)(2,1)}, bf16[128,2048]{1,0:T(8,128)(2,1)S(1)}, u32[]{:S(2)}, u32[]{:S(2)}) collective-permute-start(bf16[128,2048]{1,0:T(8,128)(2,1)} %get-tuple-element.822), channel_id=1, source_target_pairs={{32,0},{64,32},{96,64},{128,96},{160,128},{192,160},{224,192},{33,... | collective-permute-start | bytes 1572872 | tf_op jit(solution)/shard_map/while/body/eval_jaxpr/ppermute | solution.py:14
  427.7 8.3 %copy-start = (f32[2048,2048]{1,0:T(8,128)S(1)}, f32[2048,2048]{1,0:T(8,128)}, u32[]{:S(2)}) copy-start(f32[2048,2048]{1,0:T(8,128)} %get-tuple-element.558) | copy-start | bytes 50331652 | tf_op jit(solution)/shard_map/while/body/eval_jaxpr/cond
  438.9 5.7 copy-start.1
Sparse Core Ops, SparseCore 0:
  453.9 285.8 reduce-scatter.1
where the time goes:
time: 754 us; the launch traced here: 748 us
  waiting for transfers between devices  391 us (52%)
  blocking collectives  189 us (25%)
  starting transfers between devices  72.3 us (10%)
  local copies, waits for them, and re-layouts  34.1 us (5%)
  matrix products  30.2 us (4%)
  other arithmetic  17.5 us (2%)
  between operations  14.1 us (2%)
    ppermute x18, waiting for transfers between devices, shifted(): return lax.ppermute(block, axis, route)  294 us
    psum x1, blocking collectives, on_device(): g_total = lax.psum(g_local, 'dp')  189 us
    reduce_scatter x1, waiting for transfers between devices, on_device(): lax.psum_scatter(w_total.astype(jnp.bfloat16), 'dp', scatter_dimension=0,...  96.9 us
    ppermute x18, starting transfers between devices, shifted(): return lax.ppermute(block, axis, route)  72.3 us
  transfers between devices with their start and end apart: 19, of which 19 were waited for; matrix products, arithmetic and copies ran while one was open for 0% of the time, Pallas kernels for 0%

commit v1 on v0

v1 whole, which is shorter than its diff:
```python
import functools
import math

import jax
import jax.numpy as jnp
from jax import lax
from jax.experimental import pallas as pl
from jax.experimental.pallas import tpu as pltpu
from jax.sharding import PartitionSpec as P

eps = 1e-05
MESH = pl.DeviceIdType.MESH
NX = 4
CHUNK = 16
PIECES = 4
bf16 = jnp.bfloat16
f32 = jnp.float32


def kernel(
    n_section, n_dp, scale,
    inputs, cotangent, weights, gains,
    grad_in, w_out, g_out,
    w, wt, act, act_out, gath, n_send, n_gath, rinv, acc, dw,
    core_send, core_recv, z_send, z_recv, gacc, g_send, gx_recv, gc_send, gc_recv, gz_send, gz_recv,
    load_sem, w_sem, fs_sem, fr_sem, bs_sem, br_sem, xs_sem, xr_sem, ns_sem, nr_sem,
    cs_sem, cr_sem, zs_sem, zr_sem, gs_sem, gr_sem,
):
    rows, width = act.shape
    steps = rows // CHUNK
    kw = width // PIECES
    nz = n_dp // (2 * NX)
    zw = width // nz
    xw = zw // NX
    cw = xw // 2
    s = lax.axis_index("section")
    d = lax.axis_index("dp")
    core = d % 2
    x = (d // 2) % NX
    z = d // (2 * NX)
    first, last = s == 0, s == n_section - 1

    def at_x(j):
        return {"section": s, "dp": (z * NX + (x + j) % NX) * 2 + core}

    def at_z(j):
        return {"section": s, "dp": (((z + j) % nz) * NX + x) * 2 + core}

    partner = {"section": s, "dp": d + 1 - 2 * core}
    above = {"section": (s + 1) % n_section, "dp": d}
    below = {"section": (s + n_section - 1) % n_section, "dp": d}

    def remote(src, dst, send, recv, to):
        return pltpu.make_async_remote_copy(
            src_ref=src, dst_ref=dst, send_sem=send, recv_sem=recv, device_id=to, device_id_type=MESH
        )

    def w_load(k):
        part = pl.ds(k * kw, kw)
        return pltpu.make_async_copy(weights.at[part], w.at[part], w_sem.at[k])

    load_act = pltpu.make_async_copy(inputs, act, load_sem.at[0])
    load_cot = pltpu.make_async_copy(cotangent, gath.at[0], load_sem.at[1])

    @pl.when(first)
    def _():
        load_act.start()

    for k in range(PIECES):
        w_load(k).start()

    @pl.when(last)
    def _():
        load_cot.start()

    gacc[...] = jnp.zeros_like(gacc)

    barrier = pltpu.get_barrier_semaphore()
    peers = [at_x(j) for j in range(1, NX)] + [at_z(j) for j in range(1, nz)] + [partner, above, below]
    for to in peers:
        pl.semaphore_signal(barrier, inc=1, device_id=to, device_id_type=MESH)
    pl.semaphore_wait(barrier, len(peers))

    @pl.when(first)
    def _():
        load_act.wait()

    @pl.when(last)
    def _():
        load_cot.wait()

    def up(i, k):
        part = (pl.ds(pl.multiple_of(i * CHUNK, CHUNK), CHUNK), pl.ds(k * kw, kw))
        return remote(act_out.at[part], act.at[part], fs_sem.at[0], fr_sem.at[i, k], above)

    def down(i, k):
        part = (pl.ds(pl.multiple_of(i * CHUNK, CHUNK), CHUNK), pl.ds(k * kw, kw))
        return remote(grad_in.at[part], gath.at[0].at[part], bs_sem.at[0], br_sem.at[i, k], below)

    def gather(i, j):
        part = pl.ds(pl.multiple_of(i * CHUNK, CHUNK), CHUNK)
        return remote(
            gath.at[0, part], gath.at[NX - j, part], xs_sem.at[j - 1], xr_sem.at[NX - j - 1], at_x(j)
        )

    def gather_all(j):
        return remote(gath.at[0], gath.at[NX - j], xs_sem.at[j - 1], xr_sem.at[NX - j - 1], at_x(j))

    def n_gather(j):
        return remote(
            n_send.at[j - 1], n_gath.at[NX - j], ns_sem.at[j - 1], nr_sem.at[NX - j - 1], at_x(j)
        )

    def forward(i):
        part = pl.ds(pl.multiple_of(i * CHUNK, CHUNK), CHUNK)
        square = jnp.zeros((CHUNK, 1), f32)
        for k in range(PIECES):
            cols = pl.ds(k * kw, kw)

            @pl.when(jnp.logical_not(first))
            def _():
                up(i, k).wait_recv()

            a = act[part, cols].astype(f32)
            square = square + jnp.sum(a * a, axis=-1, keepdims=True)

            @pl.when(i == 0)
            def _():
                @pl.when(first)
                def _():
                    w_load(k).wait()

            @pl.when(jnp.logical_not(last))
            def _():
                b = (act[part, cols].astype(f32) * gains[:, cols]).astype(bf16)
                term = jnp.dot(b, w[cols, :], preferred_element_type=f32)
                if k == 0:
                    acc[...] = term
                else:
                    acc[...] += term

        inv = 1.0 / jnp.sqrt(square / width + eps)
        rinv[part, :] = jnp.broadcast_to(inv, (CHUNK, 128))

        @pl.when(jnp.logical_not(last))
        def _():
            for k in range(PIECES):
                cols = pl.ds(k * kw, kw)
                act_out[part, cols] = (
                    act[part, cols].astype(f32) + acc[:, k * kw : (k + 1) * kw] * inv
                ).astype(bf16)
                up(i, k).start()

        for j in range(NX):
            xj = (x + j) % NX
            for zi in range(nz):
                cols = pl.ds(pl.multiple_of(zi * zw + xj * xw, xw), xw)
                v = (act[part, cols].astype(f32) * inv * gains[:, cols]).astype(bf16)
                if j == 0:
                    n_gath[0, part, zi * xw : (zi + 1) * xw] = v
                else:
                    n_send[j - 1, part, zi * xw : (zi + 1) * xw] = v

        @pl.when(i == steps - 1)
        def _():
            for j in range(1, NX):
                n_gather(j).start()

    def backward(i):
        part = pl.ds(pl.multiple_of(i * CHUNK, CHUNK), CHUNK)
        for k in range(PIECES):
            cols = pl.ds(k * kw, kw)

            @pl.when(jnp.logical_not(last))
            def _():
                down(i, k).wait_recv()

            term = jnp.dot(gath[0, part, cols], wt[cols, :], preferred_element_type=f32)
            if k == 0:
                acc[...] = term
            else:
                acc[...] += term
        inv = rinv[part, 0:1]
        along = jnp.zeros((CHUNK, 1), f32)
        for k in range(PIECES):
            cols = slice(k * kw, (k + 1) * kw)
            along = along + jnp.sum(
                acc[:, cols] * gains[:, cols] * act[part, cols].astype(f32), axis=-1, keepdims=True
            )
        back = along * (inv * inv * inv) / width
        for k in range(PIECES):
            cols = slice(k * kw, (k + 1) * kw)
            af = act[part, cols].astype(f32)
            dn = acc[:, cols]
            grad_in[part, cols] = (
                gath[0, part, cols].astype(f32) + gains[:, cols] * dn * inv - af * back
            ).astype(bf16)

            @pl.when(jnp.logical_not(first))
            def _():
                down(i, k).start()

        for j in range(1, NX):
            gather(i, j).start()
        for k in range(PIECES):
            cols = slice(k * kw, (k + 1) * kw)
            v = acc[:, cols] * act[part, cols].astype(f32) * inv
            total = v[0:8]
            for q in range(8, CHUNK, 8):
                total = total + v[q : q + 8]
            gacc[:, cols] += total

    lead = jnp.clip(2 * (2 * (n_section - 1 - s) + 1), 1, steps)

    def step(t, carry):
        @pl.when(((t == 0) & jnp.logical_not(first)) | ((t == steps) & first))
        def _():
            @pl.when(jnp.logical_not(first))
            def _():
                for k in range(PIECES):
                    w_load(k).wait()

            side = min(256, width)
            tiles = width // side

            def flip(q, c):
                at = pl.ds(pl.multiple_of(q // tiles * side, side), side)
                to = pl.ds(pl.multiple_of(q % tiles * side, side), side)
                wt[to, at] = w[at, to].T
                return c

            lax.fori_loop(0, tiles * tiles, flip, 0)

        @pl.when(t < steps)
        def _():
            forward(t)

        @pl.when((t >= lead) & (t - lead < steps))
        def _():
            backward(t - lead)

        return carry

    lax.fori_loop(0, 2 * steps, step, 0)

    def gain_x(j):
        return remote(g_send, gx_recv.at[NX - j - 1], gs_sem.at[j - 1], gr_sem.at[NX - j - 1], at_x(j))

    def gain_z(j):
        return remote(
            gz_send, gz_recv.at[nz - j - 1], gs_sem.at[NX + j - 1], gr_sem.at[NX + nz - j - 1], at_z(j)
        )

    gain_core = remote(gc_send, gc_recv, gs_sem.at[NX - 1], gr_sem.at[NX - 1], partner)

    g_send[...] = jnp.sum(gacc[...], axis=0, keepdims=True)
    for j in range(1, NX):
        gain_x(j).start()

    for j in range(1, NX):
        gather_all(j).wait()
        n_gather(j).wait()

    def core_swap(zj):
        return remote(core_send.at[zj], core_recv.at[zj], cs_sem.at[zj], cr_sem.at[zj], partner)

    def z_swap(j):
        return remote(
            z_send.at[j - 1], z_recv.at[nz - j - 1], zs_sem.at[j - 1], zr_sem.at[nz - j - 1], at_z(j)
        )

    mine = pl.ds(pl.multiple_of(core * cw, cw), cw)
    other = pl.ds(pl.multiple_of((1 - core) * cw, cw), cw)
    order = list(range(nz - 1, 0, -1)) + [0]
    for j in order:
        zj = (z + j) % nz
        cols = pl.ds(pl.multiple_of(zj * xw, xw), xw)
        for half in range(2):
            span = slice(half * (width // 2), (half + 1) * (width // 2))
            total = None
            for q in range(NX):
                term = lax.dot_general(
                    n_gath[q, :, cols], gath[q, :, span], (((0,), (0,)), ((), ())),
                    preferred_element_type=f32,
                )
                total = term if total is None else total + term
            dw[j, :, span] = total
        core_send[j] = dw[j, other, :].astype(bf16)
        core_swap(j).start()

    for j in range(1, NX):
        gain_x(j).wait()
    total = g_send[...]
    for j in range(1, NX):
        total = total + gx_recv[j - 1]
    gc_send[...] = total
    gain_core.start()

    for j in order:
        core_swap(j).wait()
        if j:
            z_send[j - 1] = (dw[j, mine, :] + core_recv[j].astype(f32)).astype(bf16)
            z_swap(j).start()

    gain_core.wait()
    gz_send[...] = gc_send[...] + gc_recv[...]
    for j in range(1, nz):
        gain_z(j).start()

    total = dw[0, mine, :] + core_recv[0].astype(f32)
    for j in range(1, nz):
        z_swap(j).wait()
        total = total + z_recv[nz - j - 1].astype(f32)
    w_out[...] = total * scale

    total = gz_send[...]
    for j in range(1, nz):
        gain_z(j).wait()
        total = total + gz_recv[nz - j - 1]
    g_out[...] = total * scale

    @pl.when(jnp.logical_not(last))
    def _():
        remote(act_out, act, fs_sem.at[0], fr_sem.at[0, 0], above).wait_send()

    @pl.when(jnp.logical_not(first))
    def _():
        remote(grad_in, gath.at[0], bs_sem.at[0], br_sem.at[0, 0], below).wait_send()


def on_device(n_section, n_dp, inputs, cotangent, weights, gains):
    micro, tok_rows, width = inputs.shape
    rows = micro * tok_rows
    nz = n_dp // (2 * NX)
    steps = rows // CHUNK
    xw = width // nz // NX
    cw = xw // 2
    scale = 1.0 / math.sqrt(rows * n_dp)
    vmem, dma = pltpu.VMEM, pltpu.SemaphoreType.DMA
    grad_in, w_out, g_out = pl.pallas_call(
        functools.partial(kernel, n_section, n_dp, scale),
        out_shape=(
            jax.ShapeDtypeStruct((rows, width), bf16),
            jax.ShapeDtypeStruct((cw, width), f32),
            jax.ShapeDtypeStruct((1, width), f32),
        ),
        in_specs=[pl.BlockSpec(memory_space=pl.ANY)] * 3 + [pl.BlockSpec(memory_space=vmem)],
        out_specs=[pl.BlockSpec(memory_space=vmem)] * 3,
        scratch_shapes=[
            vmem((width, width), bf16),
            vmem((width, width), bf16),
            vmem((rows, width), bf16),
            vmem((rows, width), bf16),
            vmem((NX, rows, width), bf16),
            vmem((NX - 1, rows, nz * xw), bf16),
            vmem((NX, rows, nz * xw), bf16),
            vmem((rows, 128), f32),
            vmem((CHUNK, width), f32),
            vmem((nz, xw, width), f32),
            vmem((nz, cw, width), bf16),
            vmem((nz, cw, width), bf16),
            vmem((nz - 1, cw, width), bf16),
            vmem((nz - 1, cw, width), bf16),
            vmem((8, width), f32),
            vmem((1, width), f32),
            vmem((NX - 1, 1, width), f32),
            vmem((1, width), f32),
            vmem((1, width), f32),
            vmem((1, width), f32),
            vmem((nz - 1, 1, width), f32),
            dma((2,)),
            dma((PIECES,)),
            dma((1,)),
            dma((steps, PIECES)),
            dma((1,)),
            dma((steps, PIECES)),
            dma((NX - 1,)),
            dma((NX - 1,)),
            dma((NX - 1,)),
            dma((NX - 1,)),
            dma((nz,)),
            dma((nz,)),
            dma((nz - 1,)),
            dma((nz - 1,)),
            dma((NX + nz - 1,)),
            dma((NX + nz - 1,)),
        ],
        compiler_params=pltpu.CompilerParams(
            collective_id=0, has_side_effects=True, vmem_limit_bytes=56 * 1024 * 1024
        ),
        name="relay",
    )(inputs.reshape(rows, width), cotangent.reshape(rows, width), weights[0], gains)
    return grad_in.reshape(1, micro, tok_rows, width), w_out[None], g_out


def solution(mesh):
    return jax.shard_map(
        functools.partial(on_device, mesh.shape["section"], mesh.shape["dp"]),
        mesh=mesh,
        in_specs=(
            P(None, "dp", None),
            P(None, "dp", None),
            P("section", None, None),
            P("section", None),
        ),
        out_specs=(P("section", None, "dp", None), P("section", "dp", None), P("section", None)),
        check_vma=False,
    )
```

time: 754 us -> 179 us (0.24)
  waiting for transfers between devices: 391 us -> 0 us
  blocking collectives: 189 us -> 0 us
  Pallas kernels: 0 us -> 173 us
  starting transfers between devices: 72.3 us -> 0 us
  matrix products: 30.2 us -> 0 us
  local copies, waits for them, and re-layouts: 34.1 us -> 5.47 us
  other arithmetic: 17.5 us -> 0 us
  between operations: 14.1 us -> 0.64 us
    ppermute x18 -> x0, waiting for transfers between devices: 294 us -> none  [shifted(): return lax.ppermute(block, axis, route)]
    psum x1 -> x0, blocking collectives: 189 us -> none  [on_device(): g_total = lax.psum(g_local, 'dp')]
    pallas_call x0 -> x1, Pallas kernels: none -> 173 us  [on_device(): pl.pallas_call(functools.partial(kernel, n_section, n_dp, scale), out_sha...]
    reduce_scatter x1 -> x0, waiting for transfers between devices: 96.9 us -> none  [on_device(): lax.psum_scatter(w_total.astype(jnp.bfloat16), 'dp', scatter_dimension=0,...]
    ppermute x18 -> x0, starting transfers between devices: 72.3 us -> none  [shifted(): return lax.ppermute(block, axis, route)]
    dot_general x6 -> x0, matrix products: 30.2 us -> none  [the longest x2 13.3 us: backward_active(): lax.dot_general(upper, weight, (((1,), (1,)), ((), ())), preferred_elemen...]
    another operation x18 -> x0, local copies, waits for them, and re-layouts: 14.7 us -> none
    cond x8 -> x0, local copies, waits for them, and re-layouts: 11.5 us -> none
  transfers between devices with their start and end apart: 19 -> 0, of which waited for: 19 -> 0; matrix products, arithmetic and copies ran while one was open for 0% -> 0% of each run, Pallas kernels for 0% -> 0%
where the time goes in v1:
time: 179 us
  Pallas kernels  173 us (97%)
  local copies, waits for them, and re-layouts  5.47 us (3%)
    pallas_call x1, Pallas kernels, on_device(): pl.pallas_call(functools.partial(kernel, n_section, n_dp, scale), out_sha...  173 us
    unnamed x3, local copies, waits for them, and re-layouts  5.47 us

profile of v1, /device:TPU:1, one launch (start us, length us, event | category | flops | bytes accessed | tf_op | source)
XLA Modules:
  0.0 178.7 jit_solution(692280986282052622)
XLA Ops:
  0.6 172.5 %relay.1 = (bf16[256,2048]{1,0:T(8,128)(2,1)}, f32[64,2048]{1,0:T(8,128)}, f32[1,2048]{1,0:T(1,128)}) custom-call(bf16[256,2048]{1,0:T(8,128)(2,1)} %bitcast.6, bf16[256,2048]{1,0:T(8,128)(2,1)} %bitcast.7, bf16[2048,2048]{1,0:T(8,128)(2,1)} %bitcast.5, f32[1,2048]{1,0:T(1,128)} %gains.1), custom_call_target="tpu_custom_call" | custom-call | tf_op jit(solution)/shard_map/relay/pallas_call | solution.py:340
  173.2 2.3 %copy.10 = bf16[1,2,128,2048]{3,2,1,0:T(8,128)(2,1)} copy(bf16[1,2,128,2048]{3,2,1,0:T(8,128)(2,1)} %bitcast.8) | data formatting | bytes 2097152
  175.5 1.9 %copy.11 = f32[1,64,2048]{2,1,0:T(8,128)} copy(f32[1,64,2048]{2,1,0:T(8,128)} %bitcast.9) | data formatting | bytes 1048576
  177.4 1.3 copy.12

commit v2 on v1

--- a/solution.py
+++ b/solution.py
@@ -12,7 +12,11 @@
 MESH = pl.DeviceIdType.MESH
 NX = 4
 CHUNK = 16
+PIECES_UP = 2
 PIECES = 4
+GROUPS = 4
+BEHIND = 2
+AHEAD = 3
 bf16 = jnp.bfloat16
 f32 = jnp.float32
 
@@ -89,33 +93,38 @@
     def _():
         load_cot.wait()
 
+    kf = width // PIECES_UP
+
     def up(i, k):
-        part = (pl.ds(pl.multiple_of(i * CHUNK, CHUNK), CHUNK), pl.ds(k * kw, kw))
+        part = (pl.ds(pl.multiple_of(i * CHUNK, CHUNK), CHUNK), pl.ds(k * kf, kf))
         return remote(act_out.at[part], act.at[part], fs_sem.at[0], fr_sem.at[i, k], above)
 
     def down(i, k):
         part = (pl.ds(pl.multiple_of(i * CHUNK, CHUNK), CHUNK), pl.ds(k * kw, kw))
         return remote(grad_in.at[part], gath.at[0].at[part], bs_sem.at[0], br_sem.at[i, k], below)
 
-    def gather(i, j):
-        part = pl.ds(pl.multiple_of(i * CHUNK, CHUNK), CHUNK)
+    half = width // 2
+
+    def chunk(i):
+        return pl.ds(pl.multiple_of(i * CHUNK, CHUNK), CHUNK)
+
+    per_group = rows // GROUPS
+
+    def gather(part, j, group):
         return remote(
-            gath.at[0, part], gath.at[NX - j, part], xs_sem.at[j - 1], xr_sem.at[NX - j - 1], at_x(j)
+            gath.at[0, part], gath.at[NX - j, part], xs_sem.at[j - 1], xr_sem.at[NX - j - 1, group], at_x(j)
         )
 
-    def gather_all(j):
-        return remote(gath.at[0], gath.at[NX - j], xs_sem.at[j - 1], xr_sem.at[NX - j - 1], at_x(j))
-
-    def n_gather(j):
+    def n_gather(part, j):
         return remote(
-            n_send.at[j - 1], n_gath.at[NX - j], ns_sem.at[j - 1], nr_sem.at[NX - j - 1], at_x(j)
+            n_send.at[j - 1, part], n_gath.at[NX - j, part], ns_sem.at[j - 1], nr_sem.at[NX - j - 1], at_x(j)
         )
 
     def forward(i):
-        part = pl.ds(pl.multiple_of(i * CHUNK, CHUNK), CHUNK)
+        part = chunk(i)
         square = jnp.zeros((CHUNK, 1), f32)
-        for k in range(PIECES):
-            cols = pl.ds(k * kw, kw)
+        for k in range(PIECES_UP):
+            cols = pl.ds(k * kf, kf)
 
             @pl.when(jnp.logical_not(first))
             def _():
@@ -124,11 +133,10 @@
             a = act[part, cols].astype(f32)
             square = square + jnp.sum(a * a, axis=-1, keepdims=True)
 
-            @pl.when(i == 0)
+            @pl.when((i == 0) & (before == 0))
             def _():
-                @pl.when(first)
-                def _():
-                    w_load(k).wait()
+                for q in range(k * PIECES // PIECES_UP, (k + 1) * PIECES // PIECES_UP):
+                    w_load(q).wait()
 
             @pl.when(jnp.logical_not(last))
             def _():
@@ -144,10 +152,10 @@
 
         @pl.when(jnp.logical_not(last))
         def _():
-            for k in range(PIECES):
-                cols = pl.ds(k * kw, kw)
+            for k in range(PIECES_UP):
+                cols = pl.ds(k * kf, kf)
                 act_out[part, cols] = (
-                    act[part, cols].astype(f32) + acc[:, k * kw : (k + 1) * kw] * inv
+                    act[part, cols].astype(f32) + acc[:, k * kf : (k + 1) * kf] * inv
                 ).astype(bf16)
                 up(i, k).start()
 
@@ -161,13 +169,11 @@
                 else:
                     n_send[j - 1, part, zi * xw : (zi + 1) * xw] = v
 
-        @pl.when(i == steps - 1)
-        def _():
-            for j in range(1, NX):
-                n_gather(j).start()
+        for j in range(1, NX):
+            n_gather(part, j).start()
 
     def backward(i):
-        part = pl.ds(pl.multiple_of(i * CHUNK, CHUNK), CHUNK)
+        part = chunk(i)
         for k in range(PIECES):
             cols = pl.ds(k * kw, kw)
 
@@ -175,6 +181,9 @@
             def _():
                 down(i, k).wait_recv()
 
+            if k == PIECES - 1:
+                for j in (2, 1, 3):
+                    gather(part, j, i // (steps // GROUPS)).start()
             term = jnp.dot(gath[0, part, cols], wt[cols, :], preferred_element_type=f32)
             if k == 0:
                 acc[...] = term
@@ -200,8 +209,6 @@
             def _():
                 down(i, k).start()
 
-        for j in range(1, NX):
-            gather(i, j).start()
         for k in range(PIECES):
             cols = slice(k * kw, (k + 1) * kw)
             v = acc[:, cols] * act[part, cols].astype(f32) * inv
@@ -210,34 +217,85 @@
                 total = total + v[q : q + 8]
             gacc[:, cols] += total
 
-    lead = jnp.clip(2 * (2 * (n_section - 1 - s) + 1), 1, steps)
+    lead = jnp.clip(AHEAD * (2 * (n_section - 1 - s) + 1) // 2, 1, steps)
+    side = min(256, width)
+    tiles = width // side
+    before = jnp.where(s <= 1, 0, tiles * tiles)
+
+    def flip(q, c):
+        at = pl.ds(pl.multiple_of(q // tiles * side, side), side)
+        to = pl.ds(pl.multiple_of(q % tiles * side, side), side)
+        wt[to, at] = w[at, to].T
+        return c
+
+    @pl.when(before > 0)
+    def _():
+        for k in range(PIECES):
+            w_load(k).wait()
+
+    lax.fori_loop(0, before, flip, 0)
+
+    far = z >= nz // 2
+    z_m = jnp.where(far, nz - 1 - z, z)
+    edge = z_m == 0
+
+    def by_role(at_edge, inner):
+        return jnp.where(edge, at_edge, inner)
+
+    parts = [by_role(*v) for v in ((3, 2), (2, 3), (1, 0), (0, 1))]
+
+    def z_of(k):
+        return jnp.where(far, nz - 1 - k, k)
+
+    most = rows - per_group
+
+    def products(q, tail):
+        cols = pl.ds(pl.multiple_of(z_of(parts[q]) * xw, xw), xw)
+        tokens = slice(most, rows) if tail else slice(0, most)
+        for h in range(2):
+            span = slice(h * half, (h + 1) * half)
+            total = dw[q, :, span] if tail else None
+            for slot in range(NX):
+                term = lax.dot_general(
+                    n_gath[slot, tokens, cols], gath[slot, tokens, span], (((0,), (0,)), ((), ())),
+                    preferred_element_type=f32,
+                )
+                total = term if total is None else total + term
+            dw[q, :, span] = total
+
+    def group_arrived(g):
+        for j in range(1, NX):
+            gather(pl.ds(g * per_group, per_group), j, g).wait_recv()
+            if g == 0:
+                n_gather(pl.ds(0, rows), j).wait()
+
+    def most_products():
+        for g in range(GROUPS - 1):
+            group_arrived(g)
+        for q in range(nz):
+            products(q, False)
+
+    early = s < n_section // 2
 
     def step(t, carry):
-        @pl.when(((t == 0) & jnp.logical_not(first)) | ((t == steps) & first))
-        def _():
-            @pl.when(jnp.logical_not(first))
-            def _():
-                for k in range(PIECES):
-                    w_load(k).wait()
-
-            side = min(256, width)
-            tiles = width // side
-
-            def flip(q, c):
-                at = pl.ds(pl.multiple_of(q // tiles * side, side), side)
-                to = pl.ds(pl.multiple_of(q % tiles * side, side), side)
-                wt[to, at] = w[at, to].T
-                return c
-
-            lax.fori_loop(0, tiles * tiles, flip, 0)
-
         @pl.when(t < steps)
         def _():
             forward(t)
 
+        @pl.when(t == lead)
+        def _():
+            lax.fori_loop(before, tiles * tiles, flip, 0)
+
         @pl.when((t >= lead) & (t - lead < steps))
         def _():
             backward(t - lead)
+
+        due = jnp.maximum(lead + steps // GROUPS * (GROUPS - 1) - 1, steps - 1) + BEHIND
+        due = jnp.minimum(due, 2 * steps - 1)
+
+        @pl.when(early & (t == due))
+        def _():
+            most_products()
 
         return carry
 
@@ -257,36 +315,48 @@
     for j in range(1, NX):
         gain_x(j).start()
 
-    for j in range(1, NX):
-        gather_all(j).wait()
-        n_gather(j).wait()
-
-    def core_swap(zj):
-        return remote(core_send.at[zj], core_recv.at[zj], cs_sem.at[zj], cr_sem.at[zj], partner)
-
-    def z_swap(j):
-        return remote(
-            z_send.at[j - 1], z_recv.at[nz - j - 1], zs_sem.at[j - 1], zr_sem.at[nz - j - 1], at_z(j)
-        )
+    def core_swap(q):
+        return remote(core_send.at[q], core_recv.at[q], cs_sem.at[q], cr_sem.at[q], partner)
+
+    def z_send_to(q):
+        k = by_role(*((1, 2), (2, 3), (1, 0))[q])
+        slot = by_role(*((0, 3), (2, 2), (1, 1))[q])
+        to = {"section": s, "dp": (z_of(k) * NX + x) * 2 + core}
+        return remote(z_send.at[q], z_recv.at[slot], zs_sem.at[q], zr_sem.at[slot], to)
+
+    def z_arrived(slot):
+        return remote(z_send.at[0], z_recv.at[slot], zs_sem.at[0], zr_sem.at[slot], at_z(1))
 
     mine = pl.ds(pl.multiple_of(core * cw, cw), cw)
     other = pl.ds(pl.multiple_of((1 - core) * cw, cw), cw)
-    order = list(range(nz - 1, 0, -1)) + [0]
-    for j in order:
-        zj = (z + j) % nz
-        cols = pl.ds(pl.multiple_of(zj * xw, xw), xw)
-        for half in range(2):
-            span = slice(half * (width // 2), (half + 1) * (width // 2))
-            total = None
-            for q in range(NX):
-                term = lax.dot_general(
-                    n_gath[q, :, cols], gath[q, :, span], (((0,), (0,)), ((), ())),
-                    preferred_element_type=f32,
-                )
-                total = term if total is None else total + term
-            dw[j, :, span] = total
-        core_send[j] = dw[j, other, :].astype(bf16)
-        core_swap(j).start()
+
+    @pl.when(jnp.logical_not(early))
+    def _():
+        most_products()
+
+    group_arrived(GROUPS - 1)
+
+    def make(q):
+        products(q, True)
+        core_send[q] = dw[q, other, :].astype(bf16)
+        core_swap(q).start()
+
+    def pass_along(q):
+        core_swap(q).wait()
+        z_send[q] = (dw[q, mine, :] + core_recv[q].astype(f32)).astype(bf16)
+
+    make(0)
+    make(1)
+    pass_along(0)
+    z_send_to(0).start()
+    make(2)
+    make(3)
+    pass_along(1)
+    pass_along(2)
+
+    @pl.when(jnp.logical_not(edge))
+    def _():
+        z_send_to(2).start()
 
     for j in range(1, NX):
         gain_x(j).wait()
@@ -295,23 +365,35 @@
         total = total + gx_recv[j - 1]
     gc_send[...] = total
     gain_core.start()
-
-    for j in order:
-        core_swap(j).wait()
-        if j:
-            z_send[j - 1] = (dw[j, mine, :] + core_recv[j].astype(f32)).astype(bf16)
-            z_swap(j).start()
+    z_send_to(0).wait_send()
+
+    @pl.when(edge)
+    def _():
+        z_send_to(1).start()
+        z_send_to(2).start()
+
+    @pl.when(jnp.logical_not(edge))
+    def _():
+        z_arrived(0).wait_recv()
+        z_send[1] = (dw[1, mine, :] + core_recv[1].astype(f32) + z_recv[0].astype(f32)).astype(bf16)
+        z_send_to(1).start()
 
     gain_core.wait()
     gz_send[...] = gc_send[...] + gc_recv[...]
     for j in range(1, nz):
         gain_z(j).start()
 
-    total = dw[0, mine, :] + core_recv[0].astype(f32)
-    for j in range(1, nz):
-        z_swap(j).wait()
-        total = total + z_recv[nz - j - 1].astype(f32)
+    core_swap(nz - 1).wait()
+    total = dw[nz - 1, mine, :] + core_recv[nz - 1].astype(f32)
+    for slot in (1, 2):
+        z_arrived(slot).wait_recv()
+        total = total + z_recv[slot].astype(f32)
     w_out[...] = total * scale
+
+    @pl.when(jnp.logical_not(edge))
+    def _():
+        z_arrived(3).wait_recv()
+        w_out[...] += z_recv[3].astype(f32) * scale
 
     total = gz_send[...]
     for j in range(1, nz):
@@ -319,6 +401,11 @@
         total = total + gz_recv[nz - j - 1]
     g_out[...] = total * scale
 
+    for q in range(1, nz - 1):
+        z_send_to(q).wait_send()
+    for j in range(1, NX):
+        gather(pl.ds(0, rows), j, 0).wait_send()
+
     @pl.when(jnp.logical_not(last))
     def _():
         remote(act_out, act, fs_sem.at[0], fr_sem.at[0, 0], above).wait_send()
@@ -326,6 +413,27 @@
     @pl.when(jnp.logical_not(first))
     def _():
         remote(grad_in, gath.at[0], bs_sem.at[0], br_sem.at[0, 0], below).wait_send()
+
+
+def hand_over(*arrays):
+    n = len(arrays)
+
+    def copies(*refs):
+        sems = refs[2 * n]
+        moves = [pltpu.make_async_copy(refs[q], refs[n + q], sems.at[q]) for q in range(n)]
+        for move in moves:
+            move.start()
+        for move in moves:
+            move.wait()
+
+    return pl.pallas_call(
+        copies,
+        out_shape=tuple(jax.ShapeDtypeStruct(a.shape, a.dtype) for a in arrays),
+        in_specs=[pl.BlockSpec(memory_space=pl.ANY)] * n,
+        out_specs=[pl.BlockSpec(memory_space=pl.ANY)] * n,
+        scratch_shapes=[pltpu.SemaphoreType.DMA((n,))],
+        name="hand_over",
+    )(*arrays)
 
 
 def on_device(n_section, n_dp, inputs, cotangent, weights, gains):
@@ -340,9 +448,9 @@
     grad_in, w_out, g_out = pl.pallas_call(
         functools.partial(kernel, n_section, n_dp, scale),
         out_shape=(
-            jax.ShapeDtypeStruct((rows, width), bf16),
-            jax.ShapeDtypeStruct((cw, width), f32),
-            jax.ShapeDtypeStruct((1, width), f32),
+            vmem((rows, width), bf16),
+            vmem((cw, width), f32),
+            vmem((1, width), f32),
         ),
         in_specs=[pl.BlockSpec(memory_space=pl.ANY)] * 3 + [pl.BlockSpec(memory_space=vmem)],
         out_specs=[pl.BlockSpec(memory_space=vmem)] * 3,
@@ -360,7 +468,7 @@
             vmem((nz, cw, width), bf16),
             vmem((nz, cw, width), bf16),
             vmem((nz - 1, cw, width), bf16),
-            vmem((nz - 1, cw, width), bf16),
+            vmem((nz, cw, width), bf16),
             vmem((8, width), f32),
             vmem((1, width), f32),
             vmem((NX - 1, 1, width), f32),
@@ -371,17 +479,17 @@
             dma((2,)),
             dma((PIECES,)),
             dma((1,)),
-            dma((steps, PIECES)),
+            dma((steps, PIECES_UP)),
             dma((1,)),
             dma((steps, PIECES)),
             dma((NX - 1,)),
-            dma((NX - 1,)),
+            dma((NX - 1, GROUPS)),
             dma((NX - 1,)),
             dma((NX - 1,)),
             dma((nz,)),
             dma((nz,)),
             dma((nz - 1,)),
-            dma((nz - 1,)),
+            dma((nz,)),
             dma((NX + nz - 1,)),
             dma((NX + nz - 1,)),
         ],
@@ -390,6 +498,7 @@
         ),
         name="relay",
     )(inputs.reshape(rows, width), cotangent.reshape(rows, width), weights[0], gains)
+    grad_in, w_out, g_out = hand_over(grad_in, w_out, g_out)
     return grad_in.reshape(1, micro, tok_rows, width), w_out[None], g_out
 
 

time: 179 us -> 223 us (1.25)
  Pallas kernels: 173 us -> 220 us
  local copies, waits for them, and re-layouts: 5.47 us -> 2.36 us
    pallas_call x0 -> x1, Pallas kernels: none -> 49 us  [hand_over(): pl.pallas_call(copies, out_shape=tuple((jax.ShapeDtypeStruct(a.shape, a.d...]
    unnamed x3 -> x6, local copies, waits for them, and re-layouts: 5.47 us -> 2.36 us
where the time goes in v2:
time: 223 us
  Pallas kernels  220 us (99%)
  local copies, waits for them, and re-layouts  2.36 us (1%)
    pallas_call x1, Pallas kernels, on_device(): pl.pallas_call(functools.partial(kernel, n_section, n_dp, scale), out_sha...  171 us
    pallas_call x1, Pallas kernels, hand_over(): pl.pallas_call(copies, out_shape=tuple((jax.ShapeDtypeStruct(a.shape, a.d...  49 us

profile of v2, /device:TPU:1, one launch (start us, length us, event | category | flops | bytes accessed | tf_op | source)
XLA Modules:
  0.0 223.2 jit_solution(968826078946070731)
XLA Ops:
  0.6 171.2 %relay.1 = (bf16[256,2048]{1,0:T(8,128)(2,1)S(1)}, f32[64,2048]{1,0:T(8,128)S(1)}, f32[1,2048]{1,0:T(1,128)S(1)}) custom-call(bf16[256,2048]{1,0:T(8,128)(2,1)} %bitcast.6, bf16[256,2048]{1,0:T(8,128)(2,1)} %bitcast.7, bf16[2048,2048]{1,0:T(8,128)(2,1)} %bitcast.5, f32[1,2048]{1,0:T(1,128)} %gains.1), custom_call_target="tpu_custom_call" | custom-call | tf_op jit(solution)/shard_map/relay/pallas_call | solution.py:448
  171.9 0.0 copy-start
  171.9 1.0 copy-done
  172.8 0.0 copy-start.1
  172.8 0.8 copy-done.1
  173.6 0.0 copy-start.2
  173.6 0.6 copy-done.2
  174.2 49.0 %hand_over.1 = (bf16[256,2048]{1,0:T(8,128)(2,1)}, f32[64,2048]{1,0:T(8,128)}, f32[1,2048]{1,0:T(1,128)}) custom-call(bf16[256,2048]{1,0:T(8,128)(2,1)} %copy-done, f32[64,2048]{1,0:T(8,128)} %copy-done.1, f32[1,2048]{1,0:T(1,128)} %copy-done.2), custom_call_target="tpu_custom_call" | custom-call | tf_op jit(solution)/shard_map/hand_over/pallas_call | solution.py:429
Async XLA Ops:
  171.9 1.0 copy-start
  172.8 0.8 copy-start.1
  173.6 0.6 copy-start.2

commit v3 on v2

--- a/solution.py
+++ b/solution.py
@@ -16,7 +16,6 @@
 PIECES = 4
 GROUPS = 4
 BEHIND = 2
-AHEAD = 3
 bf16 = jnp.bfloat16
 f32 = jnp.float32
 
@@ -217,7 +216,8 @@
                 total = total + v[q : q + 8]
             gacc[:, cols] += total
 
-    lead = jnp.clip(AHEAD * (2 * (n_section - 1 - s) + 1) // 2, 1, steps)
+    above_me = n_section - 1 - s
+    lead = jnp.where(above_me <= 3, jnp.minimum(3 * above_me + above_me // 3, steps), steps)
     side = min(256, width)
     tiles = width // side
     before = jnp.where(s <= 1, 0, tiles * tiles)
@@ -413,27 +413,6 @@
     @pl.when(jnp.logical_not(first))
     def _():
         remote(grad_in, gath.at[0], bs_sem.at[0], br_sem.at[0, 0], below).wait_send()
-
-
-def hand_over(*arrays):
-    n = len(arrays)
-
-    def copies(*refs):
-        sems = refs[2 * n]
-        moves = [pltpu.make_async_copy(refs[q], refs[n + q], sems.at[q]) for q in range(n)]
-        for move in moves:
-            move.start()
-        for move in moves:
-            move.wait()
-
-    return pl.pallas_call(
-        copies,
-        out_shape=tuple(jax.ShapeDtypeStruct(a.shape, a.dtype) for a in arrays),
-        in_specs=[pl.BlockSpec(memory_space=pl.ANY)] * n,
-        out_specs=[pl.BlockSpec(memory_space=pl.ANY)] * n,
-        scratch_shapes=[pltpu.SemaphoreType.DMA((n,))],
-        name="hand_over",
-    )(*arrays)
 
 
 def on_device(n_section, n_dp, inputs, cotangent, weights, gains):
@@ -498,7 +477,6 @@
         ),
         name="relay",
     )(inputs.reshape(rows, width), cotangent.reshape(rows, width), weights[0], gains)
-    grad_in, w_out, g_out = hand_over(grad_in, w_out, g_out)
     return grad_in.reshape(1, micro, tok_rows, width), w_out[None], g_out
 
 

time: 223 us -> 170 us (0.76)
  Pallas kernels: 220 us -> 167 us
    pallas_call x1 -> x0, Pallas kernels: 49 us -> none  [hand_over(): pl.pallas_call(copies, out_shape=tuple((jax.ShapeDtypeStruct(a.shape, a.d...]
    pallas_call x1, Pallas kernels: 171 us -> 167 us  [on_device(): pl.pallas_call(functools.partial(kernel, n_section, n_dp, scale), out_sha...]
where the time goes in v3:
time: 170 us
  Pallas kernels  167 us (98%)
  local copies, waits for them, and re-layouts  2.36 us (1%)
    pallas_call x1, Pallas kernels, on_device(): pl.pallas_call(functools.partial(kernel, n_section, n_dp, scale), out_sha...  167 us

profile of v3, /device:TPU:1, one launch (start us, length us, event | category | flops | bytes accessed | tf_op | source)
XLA Modules:
  0.0 169.9 jit_solution(8382630686020797123)
XLA Ops:
  0.6 166.9 %relay.1 = (bf16[256,2048]{1,0:T(8,128)(2,1)S(1)}, f32[64,2048]{1,0:T(8,128)S(1)}, f32[1,2048]{1,0:T(1,128)S(1)}) custom-call(bf16[256,2048]{1,0:T(8,128)(2,1)} %bitcast.8, bf16[256,2048]{1,0:T(8,128)(2,1)} %bitcast.9, bf16[2048,2048]{1,0:T(8,128)(2,1)} %bitcast.7, f32[1,2048]{1,0:T(1,128)} %gains.1), custom_call_target="tpu_custom_call" | custom-call | tf_op jit(solution)/shard_map/relay/pallas_call | solution.py:427
  167.5 1.0 copy.10
  168.5 0.8 copy.11
  169.3 0.6 copy.12

commit v4 on v3

--- a/solution.py
+++ b/solution.py
@@ -12,7 +12,7 @@
 MESH = pl.DeviceIdType.MESH
 NX = 4
 CHUNK = 16
-PIECES_UP = 2
+PIECES_UP = 4
 PIECES = 4
 GROUPS = 4
 BEHIND = 2

time: 170 us -> 169 us (level)
  no operation moved by 1% of the time
where the time goes in v4:
time: 169 us
  Pallas kernels  166 us (98%)
  local copies, waits for them, and re-layouts  2.36 us (1%)
    pallas_call x1, Pallas kernels, on_device(): pl.pallas_call(functools.partial(kernel, n_section, n_dp, scale), out_sha...  166 us

profile of v4, /device:TPU:1, one launch (start us, length us, event | category | flops | bytes accessed | tf_op | source)
XLA Modules:
  0.0 168.7 jit_solution(5571556276163136761)
XLA Ops:
  0.6 165.7 %relay.1 = (bf16[256,2048]{1,0:T(8,128)(2,1)S(1)}, f32[64,2048]{1,0:T(8,128)S(1)}, f32[1,2048]{1,0:T(1,128)S(1)}) custom-call(bf16[256,2048]{1,0:T(8,128)(2,1)} %bitcast.8, bf16[256,2048]{1,0:T(8,128)(2,1)} %bitcast.9, bf16[2048,2048]{1,0:T(8,128)(2,1)} %bitcast.7, f32[1,2048]{1,0:T(1,128)} %gains.1), custom_call_target="tpu_custom_call" | custom-call | tf_op jit(solution)/shard_map/relay/pallas_call | solution.py:427
  166.3 1.0 copy.10
  167.3 0.8 copy.11
  168.1 0.6 copy.12
